TPU v7x, 32 devices: a whole 2x2x4 slice. The times are simulated.
32 devices in a mesh: groups: 2 (over x), vocab: 16 (over z, y, core).
Axes of the slice: x: 2, y: 2, z: 4, core: 2. Of those that a mesh axis runs over, the one named last changes fastest.
Arguments:
- hidden: bfloat16 [4096, 5376], P(('groups', 'vocab')), parts along dimension 0, may hold values from -1.5 to 1.5
- weight: bfloat16 [16384, 5376], P('vocab'), may hold values from -0.3125 to 0.3125
- lse: float32 [4096], P('groups'), parts along dimension 0, may hold values from 4 to 6.5
- loss_grad: float32 [4096], P('groups'), parts along dimension 0, may hold values from 0.5 to 8
- labels: int32 [4096], P('groups'), parts along dimension 0, may hold values from 0 to 16383, as said below
- kept_blocks: int32 [32, 3], P(('groups', 'vocab')), parts along dimension 0, may hold values from 0 to 15, as said below
- kept_count: int32 [32], P(('groups', 'vocab')), parts along dimension 0, may hold values from 1 to 3, as said below
Outputs:
- grad_hidden: bfloat16 [4096, 5376], P(('groups', 'vocab')), parts along dimension 0
- grad_weight: bfloat16 [32768, 5376], P(('groups', 'vocab')), parts along dimension 0
There are 2 independent parts, one for each index of `groups`. A program takes and returns all parts, laid end to end along the dimension named above; an argument that names none is the same for every part. Nothing has to cross between parts.
Inputs may be any that keep to these rules, and one draw needn't show every extreme that they name: `kept_blocks`: row block indices; a shard's list holds distinct row blocks, its first kept_count entries are kept and the rest are other row blocks that are not kept; every row block is kept by at least one shard. `kept_count`: some shard's count is 3 in every draw. `labels`: each token's label is an entry of a shard that keeps the token's row block.
All inputs are finite; a program needn't handle non-finite values.
Results may differ from a plain program's by a relative error of at most 0.006.
Values may be sent and summed in bfloat16 or wider, within the bound.
A program may use at most 192 MiB of HBM per device.

v0:
```python
import jax
import jax.numpy as jnp
from jax import lax
from jax.sharding import PartitionSpec as P

RB = 128


def per_device(hidden, weight, lse, loss_grad, labels, kept_blocks, kept_count):
    shards = lax.axis_size("vocab")
    my_index = lax.axis_index("vocab")
    tok_rows, feat_width = hidden.shape
    voc_rows = weight.shape[0]
    slot_count = kept_blocks.shape[1]
    sub_rows = RB // shards
    nblocks = tok_rows // sub_rows
    local_rows = hidden.reshape(nblocks, sub_rows, feat_width)
    all_lists = lax.all_gather(kept_blocks, "vocab", axis=0, tiled=True)
    own_list = kept_blocks[0]
    own_count = kept_count[0]
    label_tab = labels.reshape(shards, nblocks, sub_rows)
    lse_tab = lse.reshape(shards, nblocks, sub_rows)
    scale_tab = loss_grad.reshape(shards, nblocks, sub_rows)
    vocab_ids = my_index * voc_rows + jnp.arange(voc_rows, dtype=jnp.int32)
    block_ids = jnp.arange(nblocks, dtype=jnp.int32)

    def block_terms(slot_index, block_rows):
        row_block = own_list[slot_index]
        picked_labels = lax.dynamic_index_in_dim(label_tab, row_block, 1, keepdims=False).reshape(
            RB
        )
        picked_lse = lax.dynamic_index_in_dim(lse_tab, row_block, 1, keepdims=False).reshape(RB)
        picked_scale = lax.dynamic_index_in_dim(scale_tab, row_block, 1, keepdims=False).reshape(RB)
        logits = lax.dot_general(
            block_rows, weight, (((1,), (1,)), ((), ())), preferred_element_type=jnp.float32
        )
        onehot = (picked_labels[:, None] == vocab_ids[None, :]).astype(jnp.float32)
        keep_slot = (slot_index < own_count).astype(jnp.float32)
        factor = picked_scale * keep_slot
        block_grad = (factor[:, None] * (jnp.exp(logits - picked_lse[:, None]) - onehot)).astype(
            jnp.bfloat16
        )
        hidden_part = jnp.dot(block_grad, weight, preferred_element_type=jnp.float32).astype(
            jnp.bfloat16
        )
        update = lax.dot_general(
            block_grad, block_rows, (((0,), (0,)), ((), ())), preferred_element_type=jnp.float32
        )
        return (hidden_part, update)

    zero_w = jnp.zeros((voc_rows, feat_width), jnp.float32)

    def slot_step(slot_index, carried):
        grad_w, grad_acc = carried
        column = lax.dynamic_index_in_dim(all_lists, slot_index, 1, keepdims=False)
        outgoing = local_rows[column].reshape(shards * sub_rows, feat_width)
        block_rows = lax.all_to_all(outgoing, "vocab", split_axis=0, concat_axis=0, tiled=True)
        hidden_part, update = block_terms(slot_index, block_rows)
        returned = lax.all_to_all(hidden_part, "vocab", split_axis=0, concat_axis=0, tiled=True)
        select = (block_ids[:, None] == column[None, :]).astype(jnp.bfloat16)
        grad_acc = grad_acc + jnp.dot(
            select,
            returned.reshape(shards, sub_rows * feat_width),
            preferred_element_type=jnp.float32,
        )
        return (grad_w + update, grad_acc)

    empty_acc = jnp.zeros((nblocks, sub_rows * feat_width), jnp.float32)
    grad_w, grad_h = lax.fori_loop(0, slot_count, slot_step, (zero_w, empty_acc))
    grad_hidden = grad_h.reshape(tok_rows, feat_width).astype(jnp.bfloat16)
    return (grad_hidden, grad_w.astype(jnp.bfloat16))


def solution(mesh):
    in_specs = (
        P(("groups", "vocab"), None),
        P("vocab", None),
        P("groups"),
        P("groups"),
        P("groups"),
        P(("groups", "vocab"), None),
        P(("groups", "vocab")),
    )
    out_specs = (P(("groups", "vocab"), None), P(("groups", "vocab"), None))
    return jax.shard_map(
        per_device, mesh=mesh, in_specs=in_specs, out_specs=out_specs, check_vma=False
    )
```

profile of v0, /device:TPU:28, one launch (start us, length us, event | category | flops | bytes accessed | tf_op | source)
XLA Modules:
  0.0 313.1 jit_solution(12645887982386817189)
XLA Ops:
  0.6 16.6 %all-gather = s32[16,1,3]{2,1,0:T(1,128)S(1)} all-gather(s32[1,1,3]{2,1,0:T(1,128)} %bitcast.80), channel_id=1, replica_groups=mesh['groups'=2,'vocab'=16] {'vocab'}, dimensions={0}, use_global_device_ids=true | all-gather | bytes 204 | tf_op jit(solution)/shard_map/all_gather | solution.py:18
  17.3 0.8 reshape.67
  18.1 0.8 reshape.65
  18.9 0.8 reshape.68
  19.7 278.2 %while.16 = (s32[]{:T(128)}, f32[1024,5376]{1,0:T(8,128)}, f32[16,43008]{1,0:T(8,128)}, s32[3]{0:T(128)}, f32[16,16,8]{2,1,0:T(8,128)S(1)}, /*index=5*/s32[]{:T(...) while((s32[]{:T(128)}, f32[1024,5376]{1,0:T(8,128)}, ...), condition=%wide.region_1.2_spmd.clone, body=%wide.region_0.1_spmd.clone.sunk | while | flops 4263741696 | bytes 157701456 | solution.py:69
  19.8 3.1 gather_fusion
  22.8 8.9 %all-to-all-start = ((bf16[16,8,5376]{2,1,0:T(8,128)(2,1)}), bf16[16,8,5376]{2,1,0:T(8,128)(2,1)S(1)}, u32[]{:S(2)}, u32[]{:S(2)}) async-start(bf16[16,8,5376]{2,1,0:T(8,128)(2,1)} %gather_fusion), calls=%async_computation | async-start | bytes 2752512 | tf_op jit(solution)/shard_map/while/body/eval_jaxpr/all_to_all | solution.py:57
  32.4 0.6 dynamic_slice.58
  34.9 0.1 eq.102
  35.2 27.2 %all-to-all-done = bf16[16,8,5376]{2,1,0:T(8,128)(2,1)S(1)} async-done(((bf16[16,8,5376]{2,1,0:T(8,128)(2,1)}), bf16[16,8,5376]{2,1,0:T(8,128)(2,1)S(1)}, u32[]{:S(2)}, u32[]{:S(2)}) %all-to-all-start) | async-done | bytes 1376288 | tf_op jit(solution)/shard_map/while/body/eval_jaxpr/all_to_all | solution.py:57
  62.5 7.9 %fusion.49 = bf16[128,1024]{1,0:T(8,128)(2,1)S(1)} fusion(bf16[1024,5376]{1,0:T(8,128)(2,1)} %get-tuple-element.434, bf16[16,8,5376]{2,1,0:T(8,128)(2,1)S(1)} %all-to-all-done, s32[1024]{0:T(1024)S(1)} %iota_add_fusion.2, f32[128]{0:T(128)S(1)} %sub.57, f32[128]{0:T(128)S(1)} %mul.65, s32[128]{0:T(128)S(1)} %eq.102), kind=kOutput, calls=%fused_computation.14.clone.1 | convolution fusion | flops 1410072576 | bytes 12654080 | tf_op jit(solution)/shard_map/while/body/eval_jaxpr/dot_general | solution.py:34
  70.4 2.7 fusion.50
  73.1 6.0 %all-to-all-start.1 = ((bf16[16,8,5376]{2,1,0:T(8,128)(2,1)}), bf16[16,8,5376]{2,1,0:T(8,128)(2,1)S(1)}, u32[]{:S(2)}, u32[]{:S(2)}) async-start(bf16[16,8,5376]{2,1,0:T(8,128)(2,1)} %fusion.50), calls=%async_computation.1 | async-start | bytes 2752512 | tf_op jit(solution)/shard_map/while/body/eval_jaxpr/all_to_all | solution.py:59
  79.2 9.0 %select_add_fusion.2 = f32[1024,5376]{1,0:T(8,128)} fusion(f32[1024,5376]{1,0:T(8,128)} %get-tuple-element.412, bf16[128,1024]{1,0:T(8,128)(2,1)S(1)} %fusion.49, pred[]{:T(512)S(6)} %compare.3, bf16[16,8,5376]{2,1,0:T(8,128)(2,1)S(1)} %all-to-all-done), kind=kOutput, calls=%fused_computation.4.clone.1 | convolution fusion | flops 1420296192 | bytes 45678592 | tf_op jit(solution)/shard_map/while/body/eval_jaxpr/dot_general | solution.py:46
  88.1 21.9 %all-to-all-done.1 = bf16[16,8,5376]{2,1,0:T(8,128)(2,1)S(1)} async-done(((bf16[16,8,5376]{2,1,0:T(8,128)(2,1)}), bf16[16,8,5376]{2,1,0:T(8,128)(2,1)S(1)}, u32[]{:S(2)}, u32[]{:S(2)}) %all-to-all-start.1) | async-done | bytes 1376288 | tf_op jit(solution)/shard_map/while/body/eval_jaxpr/all_to_all | solution.py:59
  110.0 0.2 copy.23
  110.2 1.5 copy-done.1
  111.8 1.0 convolution_add_fusion.2
  112.8 1.5 copy-done.2
  114.4 3.1 gather_fusion
  117.4 6.0 %all-to-all-start = ((bf16[16,8,5376]{2,1,0:T(8,128)(2,1)}), bf16[16,8,5376]{2,1,0:T(8,128)(2,1)S(1)}, u32[]{:S(2)}, u32[]{:S(2)}) async-start(bf16[16,8,5376]{2,1,0:T(8,128)(2,1)} %gather_fusion), calls=%async_computation | async-start | bytes 2752512 | tf_op jit(solution)/shard_map/while/body/eval_jaxpr/all_to_all | solution.py:57
  124.1 0.6 dynamic_slice.58
  127.0 27.3 %all-to-all-done = bf16[16,8,5376]{2,1,0:T(8,128)(2,1)S(1)} async-done(((bf16[16,8,5376]{2,1,0:T(8,128)(2,1)}), bf16[16,8,5376]{2,1,0:T(8,128)(2,1)S(1)}, u32[]{:S(2)}, u32[]{:S(2)}) %all-to-all-start) | async-done | bytes 1376288 | tf_op jit(solution)/shard_map/while/body/eval_jaxpr/all_to_all | solution.py:57
  154.3 7.9 %fusion.49 = bf16[128,1024]{1,0:T(8,128)(2,1)S(1)} fusion(bf16[1024,5376]{1,0:T(8,128)(2,1)} %get-tuple-element.434, bf16[16,8,5376]{2,1,0:T(8,128)(2,1)S(1)} %all-to-all-done, s32[1024]{0:T(1024)S(1)} %iota_add_fusion.2, f32[128]{0:T(128)S(1)} %sub.57, f32[128]{0:T(128)S(1)} %mul.65, s32[128]{0:T(128)S(1)} %eq.102), kind=kOutput, calls=%fused_computation.14.clone.1 | convolution fusion | flops 1410072576 | bytes 12654080 | tf_op jit(solution)/shard_map/while/body/eval_jaxpr/dot_general | solution.py:34
  162.2 2.7 fusion.50
  164.9 6.0 %all-to-all-start.1 = ((bf16[16,8,5376]{2,1,0:T(8,128)(2,1)}), bf16[16,8,5376]{2,1,0:T(8,128)(2,1)S(1)}, u32[]{:S(2)}, u32[]{:S(2)}) async-start(bf16[16,8,5376]{2,1,0:T(8,128)(2,1)} %fusion.50), calls=%async_computation.1 | async-start | bytes 2752512 | tf_op jit(solution)/shard_map/while/body/eval_jaxpr/all_to_all | solution.py:59
  170.9 14.2 %select_add_fusion.2 = f32[1024,5376]{1,0:T(8,128)} fusion(f32[1024,5376]{1,0:T(8,128)} %get-tuple-element.412, bf16[128,1024]{1,0:T(8,128)(2,1)S(1)} %fusion.49, pred[]{:T(512)S(6)} %compare.3, bf16[16,8,5376]{2,1,0:T(8,128)(2,1)S(1)} %all-to-all-done), kind=kOutput, calls=%fused_computation.4.clone.1 | convolution fusion | flops 1420296192 | bytes 45678592 | tf_op jit(solution)/shard_map/while/body/eval_jaxpr/dot_general | solution.py:46
  185.1 16.6 %all-to-all-done.1 = bf16[16,8,5376]{2,1,0:T(8,128)(2,1)S(1)} async-done(((bf16[16,8,5376]{2,1,0:T(8,128)(2,1)}), bf16[16,8,5376]{2,1,0:T(8,128)(2,1)S(1)}, u32[]{:S(2)}, u32[]{:S(2)}) %all-to-all-start.1) | async-done | bytes 1376288 | tf_op jit(solution)/shard_map/while/body/eval_jaxpr/all_to_all | solution.py:59
  201.8 0.2 copy.23
  202.0 1.5 copy-done.1
  203.5 1.0 convolution_add_fusion.2
  204.6 1.5 copy-done.2
  206.1 3.1 gather_fusion
  209.2 6.0 %all-to-all-start = ((bf16[16,8,5376]{2,1,0:T(8,128)(2,1)}), bf16[16,8,5376]{2,1,0:T(8,128)(2,1)S(1)}, u32[]{:S(2)}, u32[]{:S(2)}) async-start(bf16[16,8,5376]{2,1,0:T(8,128)(2,1)} %gather_fusion), calls=%async_computation | async-start | bytes 2752512 | tf_op jit(solution)/shard_map/while/body/eval_jaxpr/all_to_all | solution.py:57
  215.9 0.6 dynamic_slice.58
  218.7 27.3 %all-to-all-done = bf16[16,8,5376]{2,1,0:T(8,128)(2,1)S(1)} async-done(((bf16[16,8,5376]{2,1,0:T(8,128)(2,1)}), bf16[16,8,5376]{2,1,0:T(8,128)(2,1)S(1)}, u32[]{:S(2)}, u32[]{:S(2)}) %all-to-all-start) | async-done | bytes 1376288 | tf_op jit(solution)/shard_map/while/body/eval_jaxpr/all_to_all | solution.py:57
  246.0 7.9 %fusion.49 = bf16[128,1024]{1,0:T(8,128)(2,1)S(1)} fusion(bf16[1024,5376]{1,0:T(8,128)(2,1)} %get-tuple-element.434, bf16[16,8,5376]{2,1,0:T(8,128)(2,1)S(1)} %all-to-all-done, s32[1024]{0:T(1024)S(1)} %iota_add_fusion.2, f32[128]{0:T(128)S(1)} %sub.57, f32[128]{0:T(128)S(1)} %mul.65, s32[128]{0:T(128)S(1)} %eq.102), kind=kOutput, calls=%fused_computation.14.clone.1 | convolution fusion | flops 1410072576 | bytes 12654080 | tf_op jit(solution)/shard_map/while/body/eval_jaxpr/dot_general | solution.py:34
  254.0 2.7 fusion.50
  256.7 6.0 %all-to-all-start.1 = ((bf16[16,8,5376]{2,1,0:T(8,128)(2,1)}), bf16[16,8,5376]{2,1,0:T(8,128)(2,1)S(1)}, u32[]{:S(2)}, u32[]{:S(2)}) async-start(bf16[16,8,5376]{2,1,0:T(8,128)(2,1)} %fusion.50), calls=%async_computation.1 | async-start | bytes 2752512 | tf_op jit(solution)/shard_map/while/body/eval_jaxpr/all_to_all | solution.py:59
  262.7 14.2 %select_add_fusion.2 = f32[1024,5376]{1,0:T(8,128)} fusion(f32[1024,5376]{1,0:T(8,128)} %get-tuple-element.412, bf16[128,1024]{1,0:T(8,128)(2,1)S(1)} %fusion.49, pred[]{:T(512)S(6)} %compare.3, bf16[16,8,5376]{2,1,0:T(8,128)(2,1)S(1)} %all-to-all-done), kind=kOutput, calls=%fused_computation.4.clone.1 | convolution fusion | flops 1420296192 | bytes 45678592 | tf_op jit(solution)/shard_map/while/body/eval_jaxpr/dot_general | solution.py:46
  276.9 16.6 %all-to-all-done.1 = bf16[16,8,5376]{2,1,0:T(8,128)(2,1)S(1)} async-done(((bf16[16,8,5376]{2,1,0:T(8,128)(2,1)}), bf16[16,8,5376]{2,1,0:T(8,128)(2,1)S(1)}, u32[]{:S(2)}, u32[]{:S(2)}) %all-to-all-start.1) | async-done | bytes 1376288 | tf_op jit(solution)/shard_map/while/body/eval_jaxpr/all_to_all | solution.py:59
  293.5 0.2 copy.23
  293.8 1.5 copy-done.1
  295.3 1.0 convolution_add_fusion.2
  296.4 1.5 copy-done.2
  297.9 1.9 convert_element_type.40
  299.8 1.5 convert_element_type.41
  301.3 11.8 %convert_element_type.42 = bf16[1024,5376]{1,0:T(8,128)(2,1)} convert(f32[1024,5376]{1,0:T(8,128)} %get-tuple-element.218) | non-fusion elementwise | flops 5505024 | bytes 33030144 | tf_op jit(solution)/shard_map/convert_element_type | solution.py:71
  (47 shorter events, 1.0 us)
Async XLA Ops:
  19.7 12.6 %copy-start.3 = (s32[3]{0:T(128)S(1)}, s32[3]{0:T(128)}, u32[]{:S(2)}) copy-start(s32[3]{0:T(128)} %get-tuple-element.429) | copy-start | bytes 40 | tf_op jit(solution)/shard_map/while
  22.8 39.7 %all-to-all-start = ((bf16[16,8,5376]{2,1,0:T(8,128)(2,1)}), bf16[16,8,5376]{2,1,0:T(8,128)(2,1)S(1)}, u32[]{:S(2)}, u32[]{:S(2)}) async-start(bf16[16,8,5376]{2,1,0:T(8,128)(2,1)} %gather_fusion), calls=%async_computation | async-start | bytes 2752512 | tf_op jit(solution)/shard_map/while/body/eval_jaxpr/all_to_all | solution.py:57
  62.5 8.0 %copy-start = (bf16[1024,5376]{1,0:T(8,128)(2,1)S(1)}, bf16[1024,5376]{1,0:T(8,128)(2,1)}, u32[]{:S(2)}) copy-start(bf16[1024,5376]{1,0:T(8,128)(2,1)} %get-tuple-element.434) | copy-start | bytes 33030148 | tf_op jit(solution)/shard_map/while
  73.1 36.8 %all-to-all-start.1 = ((bf16[16,8,5376]{2,1,0:T(8,128)(2,1)}), bf16[16,8,5376]{2,1,0:T(8,128)(2,1)S(1)}, u32[]{:S(2)}, u32[]{:S(2)}) async-start(bf16[16,8,5376]{2,1,0:T(8,128)(2,1)} %fusion.50), calls=%async_computation.1 | async-start | bytes 2752512 | tf_op jit(solution)/shard_map/while/body/eval_jaxpr/all_to_all | solution.py:59
  110.0 1.8 copy-start.1
  112.8 1.5 copy-start.2
  114.3 9.7 %copy-start.3 = (s32[3]{0:T(128)S(1)}, s32[3]{0:T(128)}, u32[]{:S(2)}) copy-start(s32[3]{0:T(128)} %get-tuple-element.429) | copy-start | bytes 40 | tf_op jit(solution)/shard_map/while
  117.4 36.8 %all-to-all-start = ((bf16[16,8,5376]{2,1,0:T(8,128)(2,1)}), bf16[16,8,5376]{2,1,0:T(8,128)(2,1)S(1)}, u32[]{:S(2)}, u32[]{:S(2)}) async-start(bf16[16,8,5376]{2,1,0:T(8,128)(2,1)} %gather_fusion), calls=%async_computation | async-start | bytes 2752512 | tf_op jit(solution)/shard_map/while/body/eval_jaxpr/all_to_all | solution.py:57
  154.3 8.0 %copy-start = (bf16[1024,5376]{1,0:T(8,128)(2,1)S(1)}, bf16[1024,5376]{1,0:T(8,128)(2,1)}, u32[]{:S(2)}) copy-start(bf16[1024,5376]{1,0:T(8,128)(2,1)} %get-tuple-element.434) | copy-start | bytes 33030148 | tf_op jit(solution)/shard_map/while
  164.9 36.8 %all-to-all-start.1 = ((bf16[16,8,5376]{2,1,0:T(8,128)(2,1)}), bf16[16,8,5376]{2,1,0:T(8,128)(2,1)S(1)}, u32[]{:S(2)}, u32[]{:S(2)}) async-start(bf16[16,8,5376]{2,1,0:T(8,128)(2,1)} %fusion.50), calls=%async_computation.1 | async-start | bytes 2752512 | tf_op jit(solution)/shard_map/while/body/eval_jaxpr/all_to_all | solution.py:59
  201.8 1.8 copy-start.1
  204.6 1.5 copy-start.2
  206.1 9.7 %copy-start.3 = (s32[3]{0:T(128)S(1)}, s32[3]{0:T(128)}, u32[]{:S(2)}) copy-start(s32[3]{0:T(128)} %get-tuple-element.429) | copy-start | bytes 40 | tf_op jit(solution)/shard_map/while
  209.2 36.8 %all-to-all-start = ((bf16[16,8,5376]{2,1,0:T(8,128)(2,1)}), bf16[16,8,5376]{2,1,0:T(8,128)(2,1)S(1)}, u32[]{:S(2)}, u32[]{:S(2)}) async-start(bf16[16,8,5376]{2,1,0:T(8,128)(2,1)} %gather_fusion), calls=%async_computation | async-start | bytes 2752512 | tf_op jit(solution)/shard_map/while/body/eval_jaxpr/all_to_all | solution.py:57
  246.0 8.0 %copy-start = (bf16[1024,5376]{1,0:T(8,128)(2,1)S(1)}, bf16[1024,5376]{1,0:T(8,128)(2,1)}, u32[]{:S(2)}) copy-start(bf16[1024,5376]{1,0:T(8,128)(2,1)} %get-tuple-element.434) | copy-start | bytes 33030148 | tf_op jit(solution)/shard_map/while
  256.7 36.8 %all-to-all-start.1 = ((bf16[16,8,5376]{2,1,0:T(8,128)(2,1)}), bf16[16,8,5376]{2,1,0:T(8,128)(2,1)S(1)}, u32[]{:S(2)}, u32[]{:S(2)}) async-start(bf16[16,8,5376]{2,1,0:T(8,128)(2,1)} %fusion.50), calls=%async_computation.1 | async-start | bytes 2752512 | tf_op jit(solution)/shard_map/while/body/eval_jaxpr/all_to_all | solution.py:59
  293.5 1.8 copy-start.1
  296.3 1.5 copy-start.2
where the time goes:
time: 316 us; the launch traced here: 313 us
  waiting for transfers between devices  137 us (43%)
  matrix products  72.3 us (23%)
  starting transfers between devices  39 us (12%)
  local copies, waits for them, and re-layouts  25.9 us (8%)
  blocking collectives  16.6 us (5%)
  other arithmetic  13.8 us (4%)
  loops' own time  7.88 us (2%)
    all_to_all x3, waiting for transfers between devices, slot_step(): lax.all_to_all(outgoing, 'vocab', split_axis=0, concat_axis=0, tiled=True)  81.8 us
    all_to_all x3, waiting for transfers between devices, slot_step(): lax.all_to_all(hidden_part, 'vocab', split_axis=0, concat_axis=0, tiled=T...  55.2 us
    dot_general x3, matrix products, block_terms(): lax.dot_general(block_grad, block_rows, (((0,), (0,)), ((), ())), preferr...  37.3 us
    dot_general x3, matrix products, block_terms(): lax.dot_general(block_rows, weight, (((1,), (1,)), ((), ())), preferred_e...  23.8 us
    all_to_all x3, starting transfers between devices, slot_step(): lax.all_to_all(outgoing, 'vocab', split_axis=0, concat_axis=0, tiled=True)  20.9 us
    all_to_all x3, starting transfers between devices, slot_step(): lax.all_to_all(hidden_part, 'vocab', split_axis=0, concat_axis=0, tiled=T...  18.1 us
    all_gather x1, blocking collectives, per_device(): all_lists = lax.all_gather(kept_blocks, 'vocab', axis=0, tiled=True)  16.6 us
    convert_element_type x1, other arithmetic, per_device(): return (grad_hidden, grad_w.astype(jnp.bfloat16))  11.8 us
  transfers between devices with their start and end apart: 6, of which 6 were waited for; matrix products, arithmetic and copies ran while one was open for 13% of the time, Pallas kernels for 0%

commit v1 on v0

--- a/solution.py
+++ b/solution.py
@@ -1,12 +1,320 @@
+import functools
+
 import jax
 import jax.numpy as jnp
 from jax import lax
+from jax.experimental import pallas as pl
+from jax.experimental.pallas import tpu as pltpu
 from jax.sharding import PartitionSpec as P
 
 RB = 128
+MESH = pl.DeviceIdType.MESH
+VMEM_CAP = 60 * 1024 * 1024
+
+
+def exchange_kernel(
+    n, rows, chunks, sw,
+    hid, w_hbm, lists, lab, lse, scl,
+    gh, g_ref, x_ref,
+    w, gw, lists_buf, out_buf, in_buf, hbuf, ret, gret, gsum, part, sel, logits,
+    w_sem, l_send, l_recv, s1_send, s1_recv, s2_send, in_recv,
+    r_send, ret_recv, gret_recv, gs_send, part_recv,
+):
+    half, quarter = n // 2, n // 4
+    cw = 2 * sw
+    me = lax.axis_index("vocab")
+    q = lax.rem(me, quarter)
+    side = lax.div(me, half)
+    hb = side * half
+    ob = half - hb
+    ml = me - hb
+    plane = lax.div(ml, quarter)
+    gate_base = quarter + side * quarter
+    gate_target = half - side * quarter + q
+    is_gate = plane == 1 - side
+    f32, bf16 = jnp.float32, jnp.bfloat16
+
+    def remote(src, dst, send, recv, to):
+        return pltpu.make_async_remote_copy(
+            src_ref=src, dst_ref=dst, send_sem=send, recv_sem=recv,
+            device_id={"vocab": to}, device_id_type=MESH,
+        )
+
+    def wait_for(ref, sem):
+        pltpu.make_async_copy(ref, ref, sem).wait()
+
+    def cols(c):
+        return pl.ds(pl.multiple_of(c * cw, 128), cw)
+
+    def subs(c, a):
+        return pl.ds(pl.multiple_of(c * cw + a * sw, 128), sw)
+
+    def peer(dd):
+        return hb + lax.rem(ml + 1 + dd, half)
+
+    def source(i):
+        return ob + i * quarter + q
+
+    barrier = pltpu.get_barrier_semaphore()
+
+    @pl.loop(1, n)
+    def _(d):
+        pl.semaphore_signal(
+            barrier, inc=1, device_id={"vocab": lax.rem(me + d, n)}, device_id_type=MESH
+        )
+
+    pl.semaphore_wait(barrier, n - 1)
+
+    def relay_copy(c):
+        return remote(
+            hid.at[:, cols(c)], gw.at[plane, c], s1_send.at[c], s1_recv.at[plane, c], gate_target
+        )
+
+    @pl.loop(0, half - 1)
+    def _(dd):
+        remote(lists, lists_buf.at[half - 2 - dd], l_send, l_recv, peer(dd)).start()
+
+    pltpu.make_async_copy(lists, lists_buf.at[half - 1], l_recv).start()
+    relay_copy(0).start()
+    relay_copy(1).start()
+    weight_copy = pltpu.make_async_copy(w_hbm, w, w_sem)
+    weight_copy.start()
+    wait_for(lists_buf, l_recv)
+    wanted = lists_buf[...].reshape(half * rows, lists.shape[1])
+    lane = lax.broadcasted_iota(jnp.int32, wanted.shape, 1)
+    sel[...] = (wanted == lane).astype(f32).astype(bf16)
+
+    def pack(value, count):
+        v = value.reshape(count, rows, cw)
+        return jnp.concatenate([v[:, :, :sw], v[:, :, sw:]], axis=1).astype(bf16)
+
+    def unpack(value, count):
+        v = value.astype(f32)
+        parts = [v[:, a * rows : (a + 1) * rows, :].reshape(count * rows, sw) for a in range(2)]
+        return [p.astype(bf16) for p in parts]
+
+    def send_rows(c, kind, block, owner):
+        picked = jnp.dot(sel[...], block, preferred_element_type=f32)
+        out_buf[c, kind] = pack(picked, half)
+
+        @pl.loop(0, half - 1)
+        def _(dd):
+            remote(
+                out_buf.at[c, kind, dd], in_buf.at[c, owner],
+                s2_send.at[c, kind], in_recv.at[c], peer(dd),
+            ).start()
+
+        pltpu.make_async_copy(
+            out_buf.at[c, kind, half - 1], in_buf.at[c, owner], in_recv.at[c]
+        ).start()
+
+    def logits_step(c):
+        wait_for(in_buf.at[c], in_recv.at[c])
+        x0, x1 = unpack(in_buf[c], n)
+        x_ref[:, subs(c, 0)] = x0
+        x_ref[:, subs(c, 1)] = x1
+        dims = (((1,), (1,)), ((), ()))
+        logits[...] += lax.dot_general(
+            x_ref[:, cols(c)], w[:, cols(c)], dims, preferred_element_type=f32
+        )
+
+    logits[...] = jnp.zeros_like(logits)
+    weight_copy.wait()
+    lag = 2
+
+    @pl.loop(0, chunks + lag)
+    def _(c):
+        @pl.when(c + 2 < chunks)
+        def _():
+            relay_copy(c + 2).start()
+
+        @pl.when(c < chunks)
+        def _():
+            send_rows(c, 0, hid[:, cols(c)], me)
+
+            @pl.when(is_gate)
+            def _():
+                @pl.loop(0, 2)
+                def _(i):
+                    wait_for(gw.at[i, c], s1_recv.at[i, c])
+                    send_rows(c, 1 + i, gw[i, c], source(i))
+
+        @pl.when(c >= lag)
+        def _():
+            logits_step(c - lag)
+
+    ids = lax.broadcasted_iota(jnp.int32, logits.shape, 1) + me * logits.shape[1]
+    onehot = (lab[...] == ids).astype(f32)
+    grad = scl[...] * (jnp.exp(logits[...] - lse[...]) - onehot)
+    g_ref[...] = jnp.where(scl[...] != 0, grad, 0.0).astype(bf16)
+
+    def gather_sum(values):
+        y = jnp.concatenate(unpack(values, half), axis=1)
+        return lax.dot_general(
+            sel[...], y, (((0,), (0,)), ((), ())), preferred_element_type=f32
+        )
+
+    @pl.loop(0, chunks + 2 * lag)
+    def _(c):
+        @pl.when(c < chunks)
+        def _():
+            hp = jnp.dot(g_ref[...], w[:, cols(c)], preferred_element_type=f32)
+            hbuf[c] = pack(hp, n)
+
+            def far(i, off):
+                qq = lax.rem(q + off, quarter)
+                gate = gate_base + qq
+                d = lax.rem(ml - (gate - hb) - 1 + half, half)
+                return remote(
+                    hbuf.at[c, ob + i * quarter + qq], gret.at[c, i, d],
+                    r_send.at[c], gret_recv.at[c, i], gate,
+                )
+
+            @pl.loop(0, 2)
+            def _(i):
+                @pl.loop(1, quarter)
+                def _(off):
+                    far(i, off).start()
+
+                @pl.when(is_gate)
+                def _():
+                    pltpu.make_async_copy(
+                        hbuf.at[c, source(i)], gret.at[c, i, half - 1], gret_recv.at[c, i]
+                    ).start()
+
+                @pl.when(jnp.logical_not(is_gate))
+                def _():
+                    far(i, 0).start()
+
+            @pl.loop(0, half - 1)
+            def _(dd):
+                remote(
+                    hbuf.at[c, peer(dd)], ret.at[c, half - 2 - dd],
+                    r_send.at[c], ret_recv.at[c], peer(dd),
+                ).start()
+
+            pltpu.make_async_copy(hbuf.at[c, me], ret.at[c, half - 1], ret_recv.at[c]).start()
+
+        @pl.when((c >= lag) & (c < chunks + lag) & is_gate)
+        def _():
+            k = c - lag
+
+            @pl.loop(0, 2)
+            def _(i):
+                wait_for(gret.at[k, i], gret_recv.at[k, i])
+                gsum[k, i] = gather_sum(gret[k, i]).astype(bf16)
+                remote(
+                    gsum.at[k, i], part.at[k], gs_send.at[k, i], part_recv.at[k], source(i)
+                ).start()
+
+        @pl.when(c >= 2 * lag)
+        def _():
+            k = c - 2 * lag
+            wait_for(ret.at[k], ret_recv.at[k])
+            near = gather_sum(ret[k])
+            wait_for(part.at[k], part_recv.at[k])
+            gh[:, cols(k)] = (near + part[k].astype(f32)).astype(bf16)
+
+    wait_for(lists_buf.at[pl.ds(0, half - 1)], l_send)
+
+    @pl.loop(0, chunks)
+    def _(c):
+        wait_for(gw.at[0, c], s1_send.at[c])
+        wait_for(out_buf.at[c, 0, pl.ds(0, half - 1)], s2_send.at[c, 0])
+
+        @pl.when(is_gate)
+        def _():
+            @pl.loop(0, 2)
+            def _(i):
+                wait_for(out_buf.at[c, 1 + i, pl.ds(0, half - 1)], s2_send.at[c, 1 + i])
+                wait_for(gsum.at[c, i], gs_send.at[c, i])
+
+            wait_for(hbuf.at[c, pl.ds(0, half + 2 * quarter - 3)], r_send.at[c])
+
+        @pl.when(jnp.logical_not(is_gate))
+        def _():
+            wait_for(hbuf.at[c, pl.ds(0, half + 2 * quarter - 1)], r_send.at[c])
+
+
+def scratch_of(n, rows, chunks, sw, toks, voc, width):
+    half = n // 2
+    bf16 = jnp.bfloat16
+    dma = pltpu.SemaphoreType.DMA
+    return [
+        pltpu.VMEM((voc, width), bf16),
+        pltpu.VMEM((2, chunks, toks, 2 * sw), bf16),
+        pltpu.VMEM((half, rows, toks), jnp.int32),
+        pltpu.VMEM((chunks, 3, half, 2 * rows, sw), bf16),
+        pltpu.VMEM((chunks, n, 2 * rows, sw), bf16),
+        pltpu.VMEM((chunks, n, 2 * rows, sw), bf16),
+        pltpu.VMEM((chunks, half, 2 * rows, sw), bf16),
+        pltpu.VMEM((chunks, 2, half, 2 * rows, sw), bf16),
+        pltpu.VMEM((chunks, 2, toks, 2 * sw), bf16),
+        pltpu.VMEM((chunks, toks, 2 * sw), bf16),
+        pltpu.VMEM((half * rows, toks), bf16),
+        pltpu.VMEM((n * rows, voc), jnp.float32),
+        dma, dma, dma,
+        dma((chunks,)), dma((2, chunks)), dma((chunks, 3)), dma((chunks,)),
+        dma((chunks,)), dma((chunks,)), dma((chunks, 2)), dma((chunks, 2)), dma((chunks,)),
+    ]
+
+
+def plan(n, tok_rows, voc, width, slots):
+    rows = slots * (RB // n)
+    if n % 4 or rows % 8 or tok_rows != 128 or width % 256:
+        return None
+    pairs = width // 256
+    chunks = min([c for c in range(1, pairs + 1) if pairs % c == 0], key=lambda c: abs(c - 7))
+    need = 2 * voc * width + 4 * n * rows * voc + 2 * n * rows * voc
+    need += 2 * width * (n * rows * 6 + tok_rows * 7)
+    if need > VMEM_CAP - 3 * 1024 * 1024:
+        return None
+    return rows, chunks, width // chunks // 2
 
 
 def per_device(hidden, weight, lse, loss_grad, labels, kept_blocks, kept_count):
+    n = lax.axis_size("vocab")
+    tok_rows, width = hidden.shape
+    voc = weight.shape[0]
+    slots = kept_blocks.shape[1]
+    planned = plan(n, tok_rows, voc, width, slots)
+    if planned is None:
+        return by_slots(hidden, weight, lse, loss_grad, labels, kept_blocks, kept_count)
+    rows, chunks, sw = planned
+    sub = RB // n
+    nblocks = tok_rows // sub
+    own = kept_blocks[0]
+    lists = own[:, None] * sub + jnp.arange(sub, dtype=jnp.int32)[None, :]
+    lists = jnp.broadcast_to(lists.reshape(rows, 1), (rows, tok_rows))
+
+    def pick(table):
+        return table.reshape(n, nblocks, sub)[:, own, :].reshape(n * rows, 1)
+
+    kept = (jnp.arange(slots, dtype=jnp.int32) < kept_count[0]).astype(jnp.float32)
+    scale = loss_grad.reshape(n, nblocks, sub)[:, own, :] * kept[None, :, None]
+    vmem = pl.BlockSpec(memory_space=pltpu.VMEM)
+    grad_h, g, x = pl.pallas_call(
+        functools.partial(exchange_kernel, n, rows, chunks, sw),
+        out_shape=(
+            jax.ShapeDtypeStruct((tok_rows, width), jnp.bfloat16),
+            jax.ShapeDtypeStruct((n * rows, voc), jnp.bfloat16),
+            jax.ShapeDtypeStruct((n * rows, width), jnp.bfloat16),
+        ),
+        in_specs=[vmem, pl.BlockSpec(memory_space=pl.ANY), vmem, vmem, vmem, vmem],
+        out_specs=(vmem, vmem, vmem),
+        scratch_shapes=scratch_of(n, rows, chunks, sw, tok_rows, voc, width),
+        compiler_params=pltpu.CompilerParams(
+            collective_id=0, has_side_effects=True, vmem_limit_bytes=VMEM_CAP
+        ),
+        name="exchange",
+    )(hidden, weight, lists, pick(labels), pick(lse), scale.reshape(n * rows, 1))
+    grad_w = lax.dot_general(
+        g, x, (((0,), (0,)), ((), ())), preferred_element_type=jnp.float32
+    )
+    return grad_h, grad_w.astype(jnp.bfloat16)
+
+
+def by_slots(hidden, weight, lse, loss_grad, labels, kept_blocks, kept_count):
     shards = lax.axis_size("vocab")
     my_index = lax.axis_index("vocab")
     tok_rows, feat_width = hidden.shape

time: 316 us -> 194 us (0.61)
  Pallas kernels: 0 us -> 171 us
  waiting for transfers between devices: 137 us -> 0 us
  matrix products: 72.3 us -> 11 us
  starting transfers between devices: 39 us -> 0 us
  local copies, waits for them, and re-layouts: 25.9 us -> 8.84 us
  blocking collectives: 16.6 us -> 0 us
  other arithmetic: 13.8 us -> 1.47 us
  loops' own time: 7.88 us -> 0 us
    pallas_call x0 -> x1, Pallas kernels: none -> 171 us  [per_device(): pl.pallas_call(functools.partial(exchange_kernel, n, rows, chunks, sw), o...]
    all_to_all x6 -> x0, waiting for transfers between devices: 137 us -> none  [the longest x3 81.8 us: slot_step(): lax.all_to_all(outgoing, 'vocab', split_axis=0, concat_axis=0, tiled=True)]
    dot_general x12 -> x1, matrix products: 72.3 us -> 11 us  [per_device(): lax.dot_general(g, x, (((0,), (0,)), ((), ())), preferred_element_type=jn...]
    all_to_all x6 -> x0, starting transfers between devices: 39 us -> none  [the longest x3 20.9 us: slot_step(): lax.all_to_all(outgoing, 'vocab', split_axis=0, concat_axis=0, tiled=True)]
    all_gather x1 -> x0, blocking collectives: 16.6 us -> none  [per_device(): all_lists = lax.all_gather(kept_blocks, 'vocab', axis=0, tiled=True)]
    convert_element_type x2 -> x1, other arithmetic: 13.7 us -> 0.01 us  [per_device(): (jnp.arange(slots, dtype=jnp.int32) < kept_count[0]).astype(jnp.float32)]
    while x27 -> x0, local copies, waits for them, and re-layouts: 9.94 us -> none
    another operation x1 -> x0, loops' own time: 7.88 us -> none  [per_device(): lax.fori_loop(0, slot_count, slot_step, (zero_w, empty_acc))]
  transfers between devices with their start and end apart: 6 -> 0, of which waited for: 6 -> 0; matrix products, arithmetic and copies ran while one was open for 13% -> 0% of each run, Pallas kernels for 0% -> 0%
where the time goes in v1:
time: 194 us; the launch traced here: 193 us
  Pallas kernels  171 us (88%)
  matrix products  11 us (6%)
  local copies, waits for them, and re-layouts  8.84 us (5%)
    pallas_call x1, Pallas kernels, per_device(): pl.pallas_call(functools.partial(exchange_kernel, n, rows, chunks, sw), o...  171 us
    dot_general x1, matrix products, per_device(): lax.dot_general(g, x, (((0,), (0,)), ((), ())), preferred_element_type=jn...  11 us

profile of v1, /device:TPU:28, one launch (start us, length us, event | category | flops | bytes accessed | tf_op | source)
XLA Modules:
  0.0 193.5 jit_solution(12650377238809414827)
XLA Ops:
  1.3 0.7 fusion
  1.9 0.7 multiply_bitcast_fusion.1
  2.6 0.1 iota_add_fusion
  2.7 0.1 add.35
  2.8 0.7 broadcast_in_dim.2.lists
  3.4 0.8 reshape.99
  4.2 0.1 copy.11
  4.3 0.5 gather_fusion.1
  4.9 0.1 copy.12
  5.0 0.8 reshape.101
  5.8 0.1 copy.13
  5.9 0.5 gather_fusion.2
  6.5 0.1 multiply_bitcast_fusion
  6.5 0.1 copy.14
  6.6 0.8 reshape.97
  7.4 0.1 copy.9
  7.5 0.5 gather_fusion
  8.1 0.1 copy.10
  8.2 0.8 reshape.126.lab
  9.0 0.8 mul.35.scl
  9.8 0.8 reshape.127.lse
  10.6 170.8 %exchange.1 = (bf16[128,5376]{1,0:T(8,128)(2,1)}, bf16[384,1024]{1,0:T(8,128)(2,1)}, bf16[384,5376]{1,0:T(8,128)(2,1)}) custom-call(bf16[128,5376]{1,0:T(8,128)(2,1)} %hid.1, bf16[1024,5376]{1,0:T(8,128)(2,1)} %w_hbm.1, s32[24,128]{1,0:T(8,128)} %broadcast_in_dim.2.lists, s32[384,1]{1,0:T(8,128)} %reshape.126.lab, f32[384,1]{1,0:T(8,128)} %reshape.127.lse, ...), custom_call_target="tpu_custom_call" | custom-call | tf_op jit(solution)/shard_map/exchange/pallas_call | solution.py:296
  181.4 0.0 copy-start
  181.4 11.0 %convolution_convert_fusion = bf16[1024,5376]{1,0:T(8,128)(2,1)} fusion(bf16[384,1024]{1,0:T(8,128)(2,1)} %get-tuple-element.6, bf16[384,5376]{1,0:T(8,128)(2,1)} %get-tuple-element.7), kind=kOutput, calls=%fused_computation.3 | convolution fusion | flops 4233363456 | bytes 15925248 | tf_op jit(solution)/shard_map/dot_general | solution.py:311
  192.4 0.0 copy-done
  192.4 1.1 copy.20
  (2 shorter events, 0.0 us)
Async XLA Ops:
  181.4 11.0 %copy-start = (bf16[128,5376]{1,0:T(8,128)(2,1)S(1)}, bf16[128,5376]{1,0:T(8,128)(2,1)}, u32[]{:S(2)}) copy-start(bf16[128,5376]{1,0:T(8,128)(2,1)} %get-tuple-element.10) | copy-start | bytes 4128772

commit v2 on v1

--- a/solution.py
+++ b/solution.py
@@ -14,10 +14,10 @@
 
 def exchange_kernel(
     n, rows, chunks, sw,
-    hid, w_hbm, lists, lab, lse, scl,
-    gh, g_ref, x_ref,
-    w, gw, lists_buf, out_buf, in_buf, hbuf, ret, gret, gsum, part, sel, logits,
-    w_sem, l_send, l_recv, s1_send, s1_recv, s2_send, in_recv,
+    hid, w_hbm, lab, lse, scl, kept_blocks, kept_count,
+    gh, gt_ref, x_hbm,
+    lists, columns, g_ref, x_ref, w, gw, lists_buf, out_buf, in_buf, hbuf, ret, gret, gsum, part, sel, logits,
+    w_sem, x_sem, l_send, l_recv, s1_send, s1_recv, s2_send, in_recv,
     r_send, ret_recv, gret_recv, gs_send, part_recv,
 ):
     half, quarter = n // 2, n // 4
@@ -55,6 +55,15 @@
     def source(i):
         return ob + i * quarter + q
 
+    sub = rows // kept_blocks.shape[1]
+    row_at = lax.broadcasted_iota(jnp.int32, lists.shape, 0)
+    lane_at = lax.broadcasted_iota(jnp.int32, lists.shape, 1)
+    slot_at = lax.div(row_at, sub)
+    source_row = lax.rem(row_at, sub)
+    for k in range(kept_blocks.shape[1]):
+        source_row += jnp.where(slot_at == k, kept_blocks[0, k] * sub, 0)
+    lists[...] = source_row
+
     barrier = pltpu.get_barrier_semaphore()
 
     @pl.loop(1, n)
@@ -79,6 +88,15 @@
     relay_copy(1).start()
     weight_copy = pltpu.make_async_copy(w_hbm, w, w_sem)
     weight_copy.start()
+    mine = source_row == lane_at
+
+    def column(table, mask):
+        spread = jnp.where(mask[None], table[:, None, :], 0.0)
+        return jnp.sum(spread, axis=-1, keepdims=True).reshape(n * rows, 1)
+
+    columns[0] = column(lab[...].astype(f32), mine)
+    columns[1] = column(lse[...], mine)
+    columns[2] = column(scl[...], mine & (slot_at < kept_count[0]))
     wait_for(lists_buf, l_recv)
     wanted = lists_buf[...].reshape(half * rows, lists.shape[1])
     lane = lax.broadcasted_iota(jnp.int32, wanted.shape, 1)
@@ -144,9 +162,12 @@
             logits_step(c - lag)
 
     ids = lax.broadcasted_iota(jnp.int32, logits.shape, 1) + me * logits.shape[1]
-    onehot = (lab[...] == ids).astype(f32)
-    grad = scl[...] * (jnp.exp(logits[...] - lse[...]) - onehot)
-    g_ref[...] = jnp.where(scl[...] != 0, grad, 0.0).astype(bf16)
+    onehot = (columns[0] == ids.astype(f32)).astype(f32)
+    scale = columns[2]
+    grad = scale * (jnp.exp(logits[...] - columns[1]) - onehot)
+    g_ref[...] = jnp.where(scale != 0, grad, 0.0).astype(bf16)
+    x_copy = pltpu.make_async_copy(x_ref, x_hbm, x_sem)
+    x_copy.start()
 
     def gather_sum(values):
         y = jnp.concatenate(unpack(values, half), axis=1)
@@ -195,6 +216,10 @@
 
             pltpu.make_async_copy(hbuf.at[c, me], ret.at[c, half - 1], ret_recv.at[c]).start()
 
+        @pl.when(c == 1)
+        def _():
+            gt_ref[...] = jnp.transpose(g_ref[...].astype(f32)).astype(bf16)
+
         @pl.when((c >= lag) & (c < chunks + lag) & is_gate)
         def _():
             k = c - lag
@@ -215,6 +240,7 @@
             wait_for(part.at[k], part_recv.at[k])
             gh[:, cols(k)] = (near + part[k].astype(f32)).astype(bf16)
 
+    x_copy.wait()
     wait_for(lists_buf.at[pl.ds(0, half - 1)], l_send)
 
     @pl.loop(0, chunks)
@@ -241,6 +267,10 @@
     bf16 = jnp.bfloat16
     dma = pltpu.SemaphoreType.DMA
     return [
+        pltpu.VMEM((rows, toks), jnp.int32),
+        pltpu.VMEM((3, n * rows, 1), jnp.float32),
+        pltpu.VMEM((n * rows, voc), bf16),
+        pltpu.VMEM((n * rows, width), bf16),
         pltpu.VMEM((voc, width), bf16),
         pltpu.VMEM((2, chunks, toks, 2 * sw), bf16),
         pltpu.VMEM((half, rows, toks), jnp.int32),
@@ -253,7 +283,7 @@
         pltpu.VMEM((chunks, toks, 2 * sw), bf16),
         pltpu.VMEM((half * rows, toks), bf16),
         pltpu.VMEM((n * rows, voc), jnp.float32),
-        dma, dma, dma,
+        dma, dma, dma, dma,
         dma((chunks,)), dma((2, chunks)), dma((chunks, 3)), dma((chunks,)),
         dma((chunks,)), dma((chunks,)), dma((chunks, 2)), dma((chunks, 2)), dma((chunks,)),
     ]
@@ -281,37 +311,56 @@
     if planned is None:
         return by_slots(hidden, weight, lse, loss_grad, labels, kept_blocks, kept_count)
     rows, chunks, sw = planned
-    sub = RB // n
-    nblocks = tok_rows // sub
-    own = kept_blocks[0]
-    lists = own[:, None] * sub + jnp.arange(sub, dtype=jnp.int32)[None, :]
-    lists = jnp.broadcast_to(lists.reshape(rows, 1), (rows, tok_rows))
-
-    def pick(table):
-        return table.reshape(n, nblocks, sub)[:, own, :].reshape(n * rows, 1)
-
-    kept = (jnp.arange(slots, dtype=jnp.int32) < kept_count[0]).astype(jnp.float32)
-    scale = loss_grad.reshape(n, nblocks, sub)[:, own, :] * kept[None, :, None]
     vmem = pl.BlockSpec(memory_space=pltpu.VMEM)
-    grad_h, g, x = pl.pallas_call(
+    smem = pl.BlockSpec(memory_space=pltpu.SMEM)
+    hbm = pl.BlockSpec(memory_space=pl.ANY)
+    tables = [t.reshape(n, tok_rows) for t in (labels, lse, loss_grad)]
+    grad_h, gt, x = pl.pallas_call(
         functools.partial(exchange_kernel, n, rows, chunks, sw),
         out_shape=(
             jax.ShapeDtypeStruct((tok_rows, width), jnp.bfloat16),
-            jax.ShapeDtypeStruct((n * rows, voc), jnp.bfloat16),
+            jax.ShapeDtypeStruct((voc, n * rows), jnp.bfloat16),
             jax.ShapeDtypeStruct((n * rows, width), jnp.bfloat16),
         ),
-        in_specs=[vmem, pl.BlockSpec(memory_space=pl.ANY), vmem, vmem, vmem, vmem],
-        out_specs=(vmem, vmem, vmem),
+        in_specs=[vmem, hbm, vmem, vmem, vmem, smem, smem],
+        out_specs=(vmem, vmem, hbm),
         scratch_shapes=scratch_of(n, rows, chunks, sw, tok_rows, voc, width),
         compiler_params=pltpu.CompilerParams(
             collective_id=0, has_side_effects=True, vmem_limit_bytes=VMEM_CAP
         ),
         name="exchange",
-    )(hidden, weight, lists, pick(labels), pick(lse), scale.reshape(n * rows, 1))
-    grad_w = lax.dot_general(
-        g, x, (((0,), (0,)), ((), ())), preferred_element_type=jnp.float32
-    )
-    return grad_h, grad_w.astype(jnp.bfloat16)
+    )(hidden, weight, *tables, kept_blocks, kept_count)
+    return grad_h, weight_gradient(gt, x, 2 * sw)
+
+
+def weight_gradient(gt, x, cw):
+    voc, depth = gt.shape
+    width = x.shape[1]
+    step = 256
+
+    def kernel(gt_ref, x_ref, out_ref):
+        for at in range(0, voc, step):
+            out_ref[at : at + step, :] = jnp.dot(
+                gt_ref[at : at + step, :], x_ref[...], preferred_element_type=jnp.float32
+            ).astype(jnp.bfloat16)
+
+    return pl.pallas_call(
+        kernel,
+        out_shape=jax.ShapeDtypeStruct((voc, width), jnp.bfloat16),
+        grid=(width // cw,),
+        in_specs=[
+            pl.BlockSpec((voc, depth), lambda i: (0, 0)),
+            pl.BlockSpec((depth, cw), lambda i: (0, i)),
+        ],
+        out_specs=pl.BlockSpec((voc, cw), lambda i: (0, i)),
+        cost_estimate=pl.CostEstimate(
+            flops=2 * voc * depth * width,
+            bytes_accessed=2 * (voc * depth + depth * width + voc * width),
+            transcendentals=0,
+        ),
+        compiler_params=pltpu.CompilerParams(vmem_limit_bytes=32 * 1024 * 1024),
+        name="weight_gradient",
+    )(gt, x)
 
 
 def by_slots(hidden, weight, lse, loss_grad, labels, kept_blocks, kept_count):

time: 194 us -> 184 us (0.948)
  matrix products: 11 us -> 0 us
  Pallas kernels: 171 us -> 178 us
  local copies, waits for them, and re-layouts: 8.84 us -> 4.38 us
    dot_general x1 -> x0, matrix products: 11 us -> none  [per_device(): lax.dot_general(g, x, (((0,), (0,)), ((), ())), preferred_element_type=jn...]
    pallas_call x0 -> x1, Pallas kernels: none -> 8.67 us  [weight_gradient(): pl.pallas_call(kernel, out_shape=jax.ShapeDtypeStruct((voc, width), jnp.b...]
    reshape x8 -> x0, local copies, waits for them, and re-layouts: 4.32 us -> none  [the longest x6 3.41 us: pick(): return table.reshape(n, nblocks, sub)[:, own, :].reshape(n * rows, 1)]
    unnamed x3 -> x7, local copies, waits for them, and re-layouts: 1.08 us -> 4.38 us
where the time goes in v2:
time: 184 us
  Pallas kernels  178 us (97%)
  local copies, waits for them, and re-layouts  4.38 us (2%)
    pallas_call x1, Pallas kernels, per_device(): pl.pallas_call(functools.partial(exchange_kernel, n, rows, chunks, sw), o...  170 us
    pallas_call x1, Pallas kernels, weight_gradient(): pl.pallas_call(kernel, out_shape=jax.ShapeDtypeStruct((voc, width), jnp.b...  8.67 us
    unnamed x7, local copies, waits for them, and re-layouts  4.38 us

profile of v2, /device:TPU:28, one launch (start us, length us, event | category | flops | bytes accessed | tf_op | source)
XLA Modules:
  0.0 183.9 jit_solution(17903000089379239327)
XLA Ops:
  1.3 169.6 %exchange.1 = (bf16[128,5376]{1,0:T(8,128)(2,1)}, bf16[1024,384]{1,0:T(8,128)(2,1)}, bf16[384,5376]{1,0:T(8,128)(2,1)}) custom-call(bf16[128,5376]{1,0:T(8,128)(2,1)} %hid.1, bf16[1024,5376]{1,0:T(8,128)(2,1)} %w_hbm.1, s32[16,128]{1,0:T(8,128)} %bitcast.3, f32[16,128]{1,0:T(8,128)} %bitcast.4, f32[16,128]{1,0:T(8,128)} %bitcast.5, s32[1,3]{1,0:T(1,128)} %kept_blocks.1, ...), custom_call_target="tpu_custom_call" | custom-call | tf_op jit(solution)/shard_map/exchange/pallas_call | solution.py:318
  170.9 0.0 copy-start
  170.9 2.2 %copy-done = bf16[384,5376]{1,0:T(8,128)(2,1)S(1)} copy-done((bf16[384,5376]{1,0:T(8,128)(2,1)S(1)}, bf16[384,5376]{1,0:T(8,128)(2,1)}, u32[]{:S(2)}) %copy-start) | copy-done | bytes 4128792
  173.1 0.0 copy-start.1
  173.1 1.1 copy-done.1
  174.2 0.0 copy-start.2
  174.2 8.7 %weight_gradient.1 = bf16[1024,5376]{1,0:T(8,128)(2,1)} custom-call(bf16[1024,384]{1,0:T(8,128)(2,1)S(1)} %copy-done.1, bf16[384,5376]{1,0:T(8,128)(2,1)S(1)} %copy-done), custom_call_target="tpu_custom_call" | custom-call | flops 4227858432 | bytes 15925248 | tf_op jit(solution)/shard_map/weight_gradient/pallas_call | solution.py:347
  182.9 0.0 copy-done.2
  182.9 1.1 copy.11
Async XLA Ops:
  170.9 2.2 %copy-start = (bf16[384,5376]{1,0:T(8,128)(2,1)S(1)}, bf16[384,5376]{1,0:T(8,128)(2,1)}, u32[]{:S(2)}) copy-start(bf16[384,5376]{1,0:T(8,128)(2,1)} %get-tuple-element.7.x_ref) | copy-start | bytes 12386308
  173.1 1.1 copy-start.1
  174.2 8.7 %copy-start.2 = (bf16[128,5376]{1,0:T(8,128)(2,1)S(1)}, bf16[128,5376]{1,0:T(8,128)(2,1)}, u32[]{:S(2)}) copy-start(bf16[128,5376]{1,0:T(8,128)(2,1)} %get-tuple-element.10) | copy-start | bytes 4128772

commit v3 on v2

--- a/solution.py
+++ b/solution.py
@@ -64,6 +64,9 @@
         source_row += jnp.where(slot_at == k, kept_blocks[0, k] * sub, 0)
     lists[...] = source_row
 
+    weight_copy = pltpu.make_async_copy(w_hbm, w, w_sem)
+    weight_copy.start()
+
     barrier = pltpu.get_barrier_semaphore()
 
     @pl.loop(1, n)
@@ -74,9 +77,14 @@
 
     pl.semaphore_wait(barrier, n - 1)
 
-    def relay_copy(c):
+    ahead, pieces = 1, 8
+    piece_rows = hid.shape[0] // pieces
+
+    def relay_copy(c, piece):
+        at = pl.ds(pl.multiple_of(piece * piece_rows, 16), piece_rows)
         return remote(
-            hid.at[:, cols(c)], gw.at[plane, c], s1_send.at[c], s1_recv.at[plane, c], gate_target
+            hid.at[at, cols(c)], gw.at[plane, c, at],
+            s1_send.at[c], s1_recv.at[plane, c], gate_target,
         )
 
     @pl.loop(0, half - 1)
@@ -84,10 +92,9 @@
         remote(lists, lists_buf.at[half - 2 - dd], l_send, l_recv, peer(dd)).start()
 
     pltpu.make_async_copy(lists, lists_buf.at[half - 1], l_recv).start()
-    relay_copy(0).start()
-    relay_copy(1).start()
-    weight_copy = pltpu.make_async_copy(w_hbm, w, w_sem)
-    weight_copy.start()
+    for c in range(1):
+        for piece in range(8):
+            relay_copy(c, piece).start()
     mine = source_row == lane_at
 
     def column(table, mask):
@@ -111,7 +118,14 @@
         parts = [v[:, a * rows : (a + 1) * rows, :].reshape(count * rows, sw) for a in range(2)]
         return [p.astype(bf16) for p in parts]
 
-    def send_rows(c, kind, block, owner):
+    def relay_piece(c, dd):
+        every = half // pieces
+
+        @pl.when((c < chunks) & (lax.rem(dd + 1, every) == 0))
+        def _():
+            relay_copy(c, lax.div(dd, every)).start()
+
+    def send_rows(c, kind, block, owner, kind_is_own):
         picked = jnp.dot(sel[...], block, preferred_element_type=f32)
         out_buf[c, kind] = pack(picked, half)
 
@@ -121,7 +135,11 @@
                 out_buf.at[c, kind, dd], in_buf.at[c, owner],
                 s2_send.at[c, kind], in_recv.at[c], peer(dd),
             ).start()
-
+            if kind_is_own:
+                relay_piece(c + ahead, dd)
+
+        if kind_is_own:
+            relay_piece(c + ahead, half - 1)
         pltpu.make_async_copy(
             out_buf.at[c, kind, half - 1], in_buf.at[c, owner], in_recv.at[c]
         ).start()
@@ -137,25 +155,24 @@
         )
 
     logits[...] = jnp.zeros_like(logits)
-    weight_copy.wait()
     lag = 2
 
     @pl.loop(0, chunks + lag)
     def _(c):
-        @pl.when(c + 2 < chunks)
-        def _():
-            relay_copy(c + 2).start()
-
         @pl.when(c < chunks)
         def _():
-            send_rows(c, 0, hid[:, cols(c)], me)
+            send_rows(c, 0, hid[:, cols(c)], me, True)
 
             @pl.when(is_gate)
             def _():
                 @pl.loop(0, 2)
                 def _(i):
                     wait_for(gw.at[i, c], s1_recv.at[i, c])
-                    send_rows(c, 1 + i, gw[i, c], source(i))
+                    send_rows(c, 1 + i, gw[i, c], source(i), False)
+
+        @pl.when(c == lag)
+        def _():
+            weight_copy.wait()
 
         @pl.when(c >= lag)
         def _():
@@ -291,7 +308,7 @@
 
 def plan(n, tok_rows, voc, width, slots):
     rows = slots * (RB // n)
-    if n % 4 or rows % 8 or tok_rows != 128 or width % 256:
+    if n % 16 or rows % 8 or tok_rows != 128 or width % 256 or voc % 256:
         return None
     pairs = width // 256
     chunks = min([c for c in range(1, pairs + 1) if pairs % c == 0], key=lambda c: abs(c - 7))
@@ -336,29 +353,59 @@
 def weight_gradient(gt, x, cw):
     voc, depth = gt.shape
     width = x.shape[1]
-    step = 256
-
-    def kernel(gt_ref, x_ref, out_ref):
-        for at in range(0, voc, step):
-            out_ref[at : at + step, :] = jnp.dot(
-                gt_ref[at : at + step, :], x_ref[...], preferred_element_type=jnp.float32
-            ).astype(jnp.bfloat16)
-
+    steps, split = width // cw, 4
+    band = voc // split
+
+    def kernel(gt_hbm, x_hbm, out_hbm, gt_ref, x_ref, out_ref, gt_sem, in_sem, out_sem):
+        gt_copy = pltpu.make_async_copy(gt_hbm, gt_ref, gt_sem)
+        gt_copy.start()
+
+        def span(i):
+            return pl.ds(i * cw, cw)
+
+        def load(i):
+            return pltpu.make_async_copy(x_hbm.at[:, span(i)], x_ref.at[:, span(i)], in_sem.at[i])
+
+        def store(i, r):
+            at = pl.ds(r * band, band)
+            return pltpu.make_async_copy(
+                out_ref.at[at, span(i)], out_hbm.at[at, span(i)], out_sem.at[i, r]
+            )
+
+        for i in range(steps):
+            load(i).start()
+        gt_copy.wait()
+        for i in range(steps):
+            load(i).wait()
+            for r in range(split):
+                at = pl.ds(r * band, band)
+                out_ref[at, span(i)] = jnp.dot(
+                    gt_ref[at, :], x_ref[:, span(i)], preferred_element_type=jnp.float32
+                ).astype(jnp.bfloat16)
+                store(i, r).start()
+        for i in range(steps):
+            for r in range(split):
+                store(i, r).wait()
+
+    hbm = pl.BlockSpec(memory_space=pl.ANY)
+    dma = pltpu.SemaphoreType.DMA
     return pl.pallas_call(
         kernel,
         out_shape=jax.ShapeDtypeStruct((voc, width), jnp.bfloat16),
-        grid=(width // cw,),
-        in_specs=[
-            pl.BlockSpec((voc, depth), lambda i: (0, 0)),
-            pl.BlockSpec((depth, cw), lambda i: (0, i)),
+        in_specs=[hbm, hbm],
+        out_specs=hbm,
+        scratch_shapes=[
+            pltpu.VMEM((voc, depth), jnp.bfloat16),
+            pltpu.VMEM((depth, width), jnp.bfloat16),
+            pltpu.VMEM((voc, width), jnp.bfloat16),
+            dma, dma((steps,)), dma((steps, split)),
         ],
-        out_specs=pl.BlockSpec((voc, cw), lambda i: (0, i)),
         cost_estimate=pl.CostEstimate(
             flops=2 * voc * depth * width,
             bytes_accessed=2 * (voc * depth + depth * width + voc * width),
             transcendentals=0,
         ),
-        compiler_params=pltpu.CompilerParams(vmem_limit_bytes=32 * 1024 * 1024),
+        compiler_params=pltpu.CompilerParams(vmem_limit_bytes=VMEM_CAP),
         name="weight_gradient",
     )(gt, x)
 

time: 184 us -> 176 us (0.957)
  Pallas kernels: 178 us -> 173 us
  local copies, waits for them, and re-layouts: 4.38 us -> 1.08 us
    pallas_call x1, Pallas kernels: 170 us -> 163 us  [per_device(): pl.pallas_call(functools.partial(exchange_kernel, n, rows, chunks, sw), o...]
    unnamed x7 -> x3, local copies, waits for them, and re-layouts: 4.38 us -> 1.08 us
where the time goes in v3:
time: 176 us
  Pallas kernels  173 us (98%)
    pallas_call x1, Pallas kernels, per_device(): pl.pallas_call(functools.partial(exchange_kernel, n, rows, chunks, sw), o...  163 us
    pallas_call x1, Pallas kernels, weight_gradient(): pl.pallas_call(kernel, out_shape=jax.ShapeDtypeStruct((voc, width), jnp.b...  10.3 us

profile of v3, /device:TPU:28, one launch (start us, length us, event | category | flops | bytes accessed | tf_op | source)
XLA Modules:
  0.0 175.7 jit_solution(13795621692284518747)
XLA Ops:
  1.3 163.0 %exchange.1 = (bf16[128,5376]{1,0:T(8,128)(2,1)}, bf16[1024,384]{1,0:T(8,128)(2,1)}, bf16[384,5376]{1,0:T(8,128)(2,1)}) custom-call(bf16[128,5376]{1,0:T(8,128)(2,1)} %hid.1, bf16[1024,5376]{1,0:T(8,128)(2,1)} %w_hbm.1, s32[16,128]{1,0:T(8,128)} %bitcast.3, f32[16,128]{1,0:T(8,128)} %bitcast.4, f32[16,128]{1,0:T(8,128)} %bitcast.5, s32[1,3]{1,0:T(1,128)} %kept_blocks.1, ...), custom_call_target="tpu_custom_call" | custom-call | tf_op jit(solution)/shard_map/exchange/pallas_call | solution.py:335
  164.3 0.0 copy-start
  164.3 10.3 %weight_gradient.1 = bf16[1024,5376]{1,0:T(8,128)(2,1)} custom-call(bf16[1024,384]{1,0:T(8,128)(2,1)} %get-tuple-element.6.gt_hbm, bf16[384,5376]{1,0:T(8,128)(2,1)} %get-tuple-element.7.x_hbm), custom_call_target="tpu_custom_call" | custom-call | flops 4227858432 | bytes 15925248 | tf_op jit(solution)/shard_map/weight_gradient/pallas_call | solution.py:392
  174.6 0.0 copy-done
  174.6 1.1 copy.11
Async XLA Ops:
  164.3 10.3 %copy-start = (bf16[128,5376]{1,0:T(8,128)(2,1)S(1)}, bf16[128,5376]{1,0:T(8,128)(2,1)}, u32[]{:S(2)}) copy-start(bf16[128,5376]{1,0:T(8,128)(2,1)} %get-tuple-element.10) | copy-start | bytes 4128772
